TPU v7x, 32 devices: a whole 2x2x4 slice. The times are simulated.
32 devices in a mesh: dp: 16 (over z, x, core), tensor: 2 (over y).
Axes of the slice: x: 2, y: 2, z: 4, core: 2. Of those that a mesh axis runs over, the one named last changes fastest.
Arguments:
- clean_images: bfloat16 [64, 256, 768], P(('dp', 'tensor')), may hold values from -6 to 6
- noise_draw: bfloat16 [64, 256, 768], P(('dp', 'tensor')), may hold values from -6 to 6
- levels: int32 [64], P(('dp', 'tensor')), may hold values from 0 to 999
- labels: int32 [64], P(('dp', 'tensor')), may hold values from 0 to 999
- dropped: int32 [64], P(('dp', 'tensor')), may hold values 0 or 1
- groups: int32 [64], P(('dp', 'tensor')), may hold values from 0 to 3
- step_count: int32 [1], replicated, may hold values from 1 to 20
- inward: float32 [1024, 3, 1024], P('dp', None, 'tensor'), may hold values from -0.1875 to 0.1875
- first_inward: float32 [1024, 3, 1024], P('dp', None, 'tensor'), may hold values from -2.744419e-06 to 2.744419e-06, as said below
- second_inward: float32 [1024, 3, 1024], P('dp', None, 'tensor'), may hold values from 3.347482e-12 to 1.3389928e-11
- outward: float32 [1024, 1024], P('tensor', 'dp'), may hold values from -0.75 to 0.75
- first_outward: float32 [1024, 1024], P('tensor', 'dp'), may hold values from -1.3722094e-06 to 1.3722094e-06, as said below
- second_outward: float32 [1024, 1024], P('tensor', 'dp'), may hold values from 8.368705e-13 to 3.347482e-12
- expand: float32 [1024, 2, 3072], P('dp', None, 'tensor'), may hold values from -0.1875 to 0.1875
- first_expand: float32 [1024, 2, 3072], P('dp', None, 'tensor'), may hold values from -1.029157e-06 to 1.029157e-06, as said below
- second_expand: float32 [1024, 2, 3072], P('dp', None, 'tensor'), may hold values from 4.7073966e-13 to 1.8829586e-12
- shrink: float32 [3072, 1024], P('tensor', 'dp'), may hold values from -0.109375 to 0.109375
- first_shrink: float32 [3072, 1024], P('tensor', 'dp'), may hold values from -2.744419e-06 to 2.744419e-06, as said below
- second_shrink: float32 [3072, 1024], P('tensor', 'dp'), may hold values from 3.347482e-12 to 1.3389928e-11
- patches: float32 [2, 768, 1024], P(None, ('dp', 'tensor')), may hold values from -0.1875 to 0.1875
- first_patches: float32 [2, 768, 1024], P(None, ('dp', 'tensor')), may hold values from -6.861047e-06 to 6.861047e-06, as said below
- second_patches: float32 [2, 768, 1024], P(None, ('dp', 'tensor')), may hold values from 2.0921763e-11 to 8.368705e-11
- classes: float32 [1001, 768], P(None, ('dp', 'tensor')), may hold values from -0.21875 to 0.21875
- first_classes: float32 [1001, 768], P(None, ('dp', 'tensor')), may hold values from -6.861047e-06 to 6.861047e-06, as said below
- second_classes: float32 [1001, 768], P(None, ('dp', 'tensor')), may hold values from 2.0921763e-11 to 8.368705e-11
- mapping: float32 [768, 4096], P(('dp', 'tensor')), may hold values from -0.21875 to 0.21875
- first_mapping: float32 [768, 4096], P(('dp', 'tensor')), may hold values from -6.861047e-06 to 6.861047e-06, as said below
- second_mapping: float32 [768, 4096], P(('dp', 'tensor')), may hold values from 2.0921763e-11 to 8.368705e-11
Outputs:
- total_loss: float32 [], replicated
- grad_norm: float32 [], replicated
- inward_next: float32 [1024, 3, 1024], P('dp', None, 'tensor')
- moment_inward: float32 [1024, 3, 1024], P('dp', None, 'tensor')
- square_inward: float32 [1024, 3, 1024], P('dp', None, 'tensor')
- outward_next: float32 [1024, 1024], P('tensor', 'dp')
- moment_outward: float32 [1024, 1024], P('tensor', 'dp')
- square_outward: float32 [1024, 1024], P('tensor', 'dp')
- expand_next: float32 [1024, 2, 3072], P('dp', None, 'tensor')
- moment_expand: float32 [1024, 2, 3072], P('dp', None, 'tensor')
- square_expand: float32 [1024, 2, 3072], P('dp', None, 'tensor')
- shrink_next: float32 [3072, 1024], P('tensor', 'dp')
- moment_shrink: float32 [3072, 1024], P('tensor', 'dp')
- square_shrink: float32 [3072, 1024], P('tensor', 'dp')
- patches_next: float32 [2, 768, 1024], P(None, ('dp', 'tensor'))
- moment_patches: float32 [2, 768, 1024], P(None, ('dp', 'tensor'))
- square_patches: float32 [2, 768, 1024], P(None, ('dp', 'tensor'))
- classes_next: float32 [1001, 768], P(None, ('dp', 'tensor'))
- moment_classes: float32 [1001, 768], P(None, ('dp', 'tensor'))
- square_classes: float32 [1001, 768], P(None, ('dp', 'tensor'))
- mapping_next: float32 [768, 4096], P(('dp', 'tensor'))
- moment_mapping: float32 [768, 4096], P(('dp', 'tensor'))
- square_mapping: float32 [768, 4096], P(('dp', 'tensor'))
Inputs may be any that keep to these rules, and one draw needn't show every extreme that they name: `first_inward`: entries of both signs. `first_outward`: entries of both signs. `first_expand`: entries of both signs. `first_shrink`: entries of both signs. `first_patches`: entries of both signs. `first_classes`: entries of both signs. `first_mapping`: entries of both signs.
All inputs are finite; a program needn't handle non-finite values. No bound on the sum of `dropped` on one device may be relied on, other than what follows from the above.
Results may differ from a plain program's by a relative error of at most 0.012.
Values may be sent and summed in bfloat16 or wider, within the bound.
No kernel may reach another device: no remote copies, remote signals or barrier semaphores. Data moves between devices by JAX's collectives and lax.ppermute only.
A program may use at most 256 MiB of HBM per device.

v0:
```python
import math
import jax
import jax.numpy as jnp
from jax import lax
from jax.sharding import PartitionSpec as P

D = 1024
HEAD_DIM = 64
CD = 768
CLASSES = 1001
PD = 768
FOUR = 256
SEQ = 256
GROUPS = 4
NLEVELS = 1000
HIGH = lax.Precision.HIGHEST
SIGMA_DATA = 0.5
LEARN_RATE = 0.05
DECAY = 0.1
BETA_ONE = 0.5
BETA_TWO = 0.5
ADAM_EPS = 1e-08
CLIP = 0.02
NORM_EPS = 1e-06


def to_low(value):
    return value.astype(jnp.bfloat16).astype(jnp.float32)


def rms_norm(value):
    return value * lax.rsqrt(jnp.mean(value * value, axis=-1, keepdims=True) + NORM_EPS)


def einsum_low(form, left, right):
    return jnp.einsum(form, left, right, preferred_element_type=jnp.float32)


def outer_sum(left, right):
    return jnp.dot(left.T, right, precision=HIGH)


def noise_terms(levels):
    log_sigma = -3.0 + 6.0 * levels.astype(jnp.float32) / (NLEVELS - 1)
    sigma = jnp.exp(log_sigma)
    radius = jnp.sqrt(sigma * sigma + SIGMA_DATA * SIGMA_DATA)
    half = FOUR // 2
    freqs = jnp.exp(-2.0 + 4.0 * jnp.arange(half, dtype=jnp.float32) / (half - 1))
    angles = 2.0 * math.pi * (log_sigma / 4.0)[:, None] * freqs[None, :]
    return (sigma, radius, jnp.concatenate([jnp.cos(angles), jnp.sin(angles)], axis=1))


def map_forward(feats, onehot, table, mats):
    feats_low = to_low(feats)
    cond_zero = jnp.dot(onehot, table, precision=HIGH) + jnp.dot(
        feats_low, mats[:, :FOUR].T, precision=HIGH
    )
    normed = to_low(rms_norm(cond_zero))
    inner = jnp.dot(normed, mats[:, FOUR : FOUR + CD], precision=HIGH)
    cond_low = to_low(cond_zero + jax.nn.gelu(inner))
    scales = 1.0 + jnp.dot(cond_low, mats[:, FOUR + CD :], precision=HIGH)
    return (scales, (feats_low, cond_zero, normed, inner, cond_low))


def map_backward(mats, kept, grad_scales):
    feats_low, cond_zero, normed, inner, cond_low = kept
    grad_cond = jnp.dot(grad_scales, mats[:, FOUR + CD :].T, precision=HIGH)
    _, pull_gelu = jax.vjp(jax.nn.gelu, inner)
    (grad_inner,) = pull_gelu(grad_cond)
    grad_normed = jnp.dot(grad_inner, mats[:, FOUR : FOUR + CD].T, precision=HIGH)
    _, pull_norm = jax.vjp(rms_norm, cond_zero)
    (grad_zero,) = pull_norm(grad_normed)
    return (grad_zero + grad_cond, grad_inner)


def scale_norm(hidden, scale):
    return rms_norm(hidden) * scale[:, None, :]


def norm_back(hidden, scale, grad):
    _, pull = jax.vjp(scale_norm, hidden, scale)
    return pull(grad)


def pair_rows(value):
    return lax.all_gather(value, "tensor", axis=0, tiled=True)


def pair_sum(value):
    return lax.psum_scatter(value, "tensor", scatter_dimension=0, tiled=True)


def split_heads(project):
    images, tokens = (project.shape[0], project.shape[1])
    heads = project.shape[3] // HEAD_DIM
    return tuple(
        (project[:, :, part].reshape(images, tokens, heads, HEAD_DIM) for part in range(3))
    )


def attention_probs(queries, keys, totals):
    scores = einsum_low("iqhe,ikhe->ihqk", queries, keys) * (1.0 / math.sqrt(HEAD_DIM))
    return jnp.exp(scores - totals)


def layer_forward(big, patch_pair, inputs, scales):
    attn_in, attn_out, gate_up, down = big
    resid_zero = einsum_low("isp,pd->isd", inputs, patch_pair[0])
    rows_zero = pair_rows(scale_norm(resid_zero, scales[:, 0]).astype(jnp.bfloat16))
    project = einsum_low("isd,dke->iske", rows_zero, attn_in).astype(jnp.bfloat16)
    queries, keys, values = split_heads(project)
    scores = einsum_low("iqhe,ikhe->ihqk", queries, keys) * (1.0 / math.sqrt(HEAD_DIM))
    totals = jax.nn.logsumexp(scores, axis=-1, keepdims=True)
    probs = jnp.exp(scores - totals).astype(jnp.bfloat16)
    mixed = einsum_low("ihqk,ikhe->iqhe", probs, values).astype(jnp.bfloat16)
    mixed = mixed.reshape(mixed.shape[0], mixed.shape[1], -1)
    resid_one = resid_zero + pair_sum(einsum_low("isd,de->ise", mixed, attn_out))
    rows_one = pair_rows(scale_norm(resid_one, scales[:, 1]).astype(jnp.bfloat16))
    gated = einsum_low("isd,dkf->iskf", rows_one, gate_up)
    hidden = (jax.nn.gelu(gated[:, :, 0]) * gated[:, :, 1]).astype(jnp.bfloat16)
    resid_two = resid_one + pair_sum(einsum_low("isf,fd->isd", hidden, down))
    last = scale_norm(resid_two, scales[:, 2]).astype(jnp.bfloat16)
    output = einsum_low("isd,pd->isp", last, patch_pair[1])
    return (
        resid_zero,
        rows_zero,
        project,
        totals,
        mixed,
        resid_one,
        rows_one,
        gated,
        hidden,
        resid_two,
        last,
        output,
    )


def layer_backward(big, patch_pair, inputs, scales, kept, grad_out):
    attn_in, attn_out, gate_up, down = big
    (
        resid_zero,
        rows_zero,
        project,
        totals,
        mixed,
        resid_one,
        rows_one,
        gated,
        hidden,
        resid_two,
        last,
        output,
    ) = kept
    grad_low = grad_out.astype(jnp.bfloat16)
    grad_last = einsum_low("isp,pd->isd", grad_low, patch_pair[1])
    grad_patch_out = einsum_low("isp,isd->pd", grad_low, last)
    grad_two, scale_two = norm_back(resid_two, scales[:, 2], grad_last)
    rows_grad = pair_rows(grad_two.astype(jnp.bfloat16))
    grad_hidden = einsum_low("isd,fd->isf", rows_grad, down)
    grad_down = einsum_low("isf,isd->fd", hidden, rows_grad)
    _, pull_gate = jax.vjp(
        lambda gate, upper: jax.nn.gelu(gate) * upper, gated[:, :, 0], gated[:, :, 1]
    )
    grad_gate, grad_up = pull_gate(grad_hidden)
    grad_gated = jnp.stack([grad_gate, grad_up], axis=2).astype(jnp.bfloat16)
    grad_gate_up = einsum_low("isd,iskf->dkf", rows_one, grad_gated)
    part_one, scale_one = norm_back(
        resid_one, scales[:, 1], pair_sum(einsum_low("iskf,dkf->isd", grad_gated, gate_up))
    )
    grad_one = grad_two + part_one
    rows_grad = pair_rows(grad_one.astype(jnp.bfloat16))
    queries, keys, values = split_heads(project)
    grad_mixed = (
        einsum_low("isd,ed->ise", rows_grad, attn_out).astype(jnp.bfloat16).reshape(queries.shape)
    )
    grad_attn_out = einsum_low("ise,isd->ed", mixed, rows_grad)
    probs = attention_probs(queries, keys, totals)
    grad_values = einsum_low("ihqk,iqhe->ikhe", probs.astype(jnp.bfloat16), grad_mixed)
    grad_probs = einsum_low("iqhe,ikhe->ihqk", grad_mixed, values)
    grad_scores = (
        probs * (grad_probs - jnp.sum(grad_probs * probs, axis=-1, keepdims=True))
    ).astype(jnp.bfloat16)
    inverse_root = 1.0 / math.sqrt(HEAD_DIM)
    grad_queries = einsum_low("ihqk,ikhe->iqhe", grad_scores, keys) * inverse_root
    grad_keys = einsum_low("ihqk,iqhe->ikhe", grad_scores, queries) * inverse_root
    grad_project = jnp.stack([grad_queries, grad_keys, grad_values], axis=2)
    grad_project = grad_project.reshape(project.shape).astype(jnp.bfloat16)
    grad_attn_in = einsum_low("isd,iske->dke", rows_zero, grad_project)
    part_zero, scale_zero = norm_back(
        resid_zero, scales[:, 0], pair_sum(einsum_low("iske,dke->isd", grad_project, attn_in))
    )
    grad_zero = (grad_one + part_zero).astype(jnp.bfloat16)
    grad_patch_in = einsum_low("isp,isd->pd", inputs, grad_zero)
    grad_scales = jnp.stack([scale_zero, scale_one, scale_two], axis=1)
    return (
        (grad_attn_in, grad_attn_out, grad_gate_up, grad_down),
        jnp.stack([grad_patch_in, grad_patch_out]),
        grad_scales,
    )


def body(
    clean_images,
    noise_draw,
    levels,
    labels,
    dropped,
    groups,
    step_count,
    inward,
    first_inward,
    second_inward,
    outward,
    first_outward,
    second_outward,
    expand,
    first_expand,
    second_expand,
    shrink,
    first_shrink,
    second_shrink,
    patches,
    first_patches,
    second_patches,
    classes,
    first_classes,
    second_classes,
    mapping,
    first_mapping,
    second_mapping,
):
    masters = (inward, outward, expand, shrink, patches, classes, mapping)
    firsts = (
        first_inward,
        first_outward,
        first_expand,
        first_shrink,
        first_patches,
        first_classes,
        first_mapping,
    )
    seconds = (
        second_inward,
        second_outward,
        second_expand,
        second_shrink,
        second_patches,
        second_classes,
        second_mapping,
    )
    big = (
        lax.all_gather(inward.astype(jnp.bfloat16), "dp", axis=0, tiled=True),
        lax.all_gather(outward.astype(jnp.bfloat16), "dp", axis=1, tiled=True),
        lax.all_gather(expand.astype(jnp.bfloat16), "dp", axis=0, tiled=True),
        lax.all_gather(shrink.astype(jnp.bfloat16), "dp", axis=1, tiled=True),
    )
    small = (
        lax.all_gather(patches.astype(jnp.bfloat16), ("dp", "tensor"), axis=1, tiled=True),
        lax.all_gather(classes.astype(jnp.bfloat16), ("dp", "tensor"), axis=1, tiled=True),
        lax.all_gather(mapping.astype(jnp.bfloat16), ("dp", "tensor"), axis=0, tiled=True),
    )
    sigma, radius, feats = noise_terms(levels)
    chosen = jnp.where(dropped == 1, CLASSES - 1, labels)
    onehot = (chosen[:, None] == jnp.arange(CLASSES)[None, :]).astype(jnp.float32)
    map_mats = small[2].astype(jnp.float32)
    scale_flat, map_kept = map_forward(feats, onehot, small[1].astype(jnp.float32), map_mats)
    scales = scale_flat.reshape(-1, 3, D)
    sig = sigma[:, None, None]
    rad = radius[:, None, None]
    clean_float = clean_images.astype(jnp.float32)
    noise_float = noise_draw.astype(jnp.float32)
    inputs = ((clean_float + sig * noise_float) / rad).astype(jnp.bfloat16)
    target = (sig * clean_float - SIGMA_DATA * SIGMA_DATA * noise_float) / (SIGMA_DATA * rad)
    kept = layer_forward(big, small[0], inputs, scales)
    output = kept[-1]
    counts = jnp.sum((groups[:, None] == groups[None, :]).astype(jnp.float32), axis=1)
    weight = 1.0 / (GROUPS * counts)
    local_loss = jnp.sum(weight * jnp.mean((output - target) ** 2, axis=(1, 2)))
    total_loss = lax.psum(local_loss, ("dp", "tensor"))
    grad_out = 2.0 * (output - target) * (weight / (SEQ * PD))[:, None, None]
    backward_big = (
        lax.all_gather(inward.astype(jnp.bfloat16), "dp", axis=0, tiled=True),
        lax.all_gather(outward.astype(jnp.bfloat16), "dp", axis=1, tiled=True),
        lax.all_gather(expand.astype(jnp.bfloat16), "dp", axis=0, tiled=True),
        lax.all_gather(shrink.astype(jnp.bfloat16), "dp", axis=1, tiled=True),
    )
    big_grads, patch_grads, scale_grads = layer_backward(
        backward_big, small[0], inputs, scales, kept, grad_out
    )
    grad_scales = scale_grads.reshape(-1, 3 * D)
    grad_zero, grad_inner = map_backward(map_mats, map_kept, grad_scales)
    feats_low, cond_zero, normed, inner, cond_low = map_kept
    big_shards = (
        lax.psum_scatter(big_grads[0], "dp", scatter_dimension=0, tiled=True),
        lax.psum_scatter(big_grads[1], "dp", scatter_dimension=1, tiled=True),
        lax.psum_scatter(big_grads[2], "dp", scatter_dimension=0, tiled=True),
        lax.psum_scatter(big_grads[3], "dp", scatter_dimension=1, tiled=True),
    )
    table_grad = outer_sum(onehot, grad_zero)
    mapping_grad = jnp.concatenate(
        [
            outer_sum(grad_zero, feats_low),
            outer_sum(normed, grad_inner),
            outer_sum(cond_low, grad_scales),
        ],
        axis=1,
    )
    small_shards = (
        lax.psum_scatter(patch_grads, ("dp", "tensor"), scatter_dimension=1, tiled=True),
        lax.psum_scatter(table_grad, ("dp", "tensor"), scatter_dimension=1, tiled=True),
        lax.psum_scatter(mapping_grad, ("dp", "tensor"), scatter_dimension=0, tiled=True),
    )
    grads = tuple(big_shards) + tuple(small_shards)
    squares = sum((jnp.sum(grad * grad) for grad in grads))
    squares_total = lax.psum(squares, ("dp", "tensor"))
    grad_norm = jnp.sqrt(squares_total)
    factor = CLIP / (grad_norm + NORM_EPS)
    count = step_count[0].astype(jnp.float32)
    fix_one = 1.0 - jnp.power(BETA_ONE, count)
    fix_two = 1.0 - jnp.power(BETA_TWO, count)
    results = [total_loss, grad_norm]
    for master, first, second, grad in zip(masters, firsts, seconds, grads):
        clipped = grad * factor
        moment = BETA_ONE * first + (1.0 - BETA_ONE) * clipped
        square = BETA_TWO * second + (1.0 - BETA_TWO) * clipped * clipped
        step_size = moment / fix_one / (jnp.sqrt(square / fix_two) + ADAM_EPS)
        results.extend([master - LEARN_RATE * (step_size + DECAY * master), moment, square])
    return tuple(results)


def solution(mesh):
    in_specs = (
        P(("dp", "tensor"), None, None),
        P(("dp", "tensor"), None, None),
        P(("dp", "tensor")),
        P(("dp", "tensor")),
        P(("dp", "tensor")),
        P(("dp", "tensor")),
        P(),
        P("dp", None, "tensor"),
        P("dp", None, "tensor"),
        P("dp", None, "tensor"),
        P("tensor", "dp"),
        P("tensor", "dp"),
        P("tensor", "dp"),
        P("dp", None, "tensor"),
        P("dp", None, "tensor"),
        P("dp", None, "tensor"),
        P("tensor", "dp"),
        P("tensor", "dp"),
        P("tensor", "dp"),
        P(None, ("dp", "tensor"), None),
        P(None, ("dp", "tensor"), None),
        P(None, ("dp", "tensor"), None),
        P(None, ("dp", "tensor")),
        P(None, ("dp", "tensor")),
        P(None, ("dp", "tensor")),
        P(("dp", "tensor"), None),
        P(("dp", "tensor"), None),
        P(("dp", "tensor"), None),
    )
    out_specs = (
        P(),
        P(),
        P("dp", None, "tensor"),
        P("dp", None, "tensor"),
        P("dp", None, "tensor"),
        P("tensor", "dp"),
        P("tensor", "dp"),
        P("tensor", "dp"),
        P("dp", None, "tensor"),
        P("dp", None, "tensor"),
        P("dp", None, "tensor"),
        P("tensor", "dp"),
        P("tensor", "dp"),
        P("tensor", "dp"),
        P(None, ("dp", "tensor"), None),
        P(None, ("dp", "tensor"), None),
        P(None, ("dp", "tensor"), None),
        P(None, ("dp", "tensor")),
        P(None, ("dp", "tensor")),
        P(None, ("dp", "tensor")),
        P(("dp", "tensor"), None),
        P(("dp", "tensor"), None),
        P(("dp", "tensor"), None),
    )
    return jax.shard_map(body, mesh=mesh, in_specs=in_specs, out_specs=out_specs, check_vma=False)
```

profile of v0, /device:TPU:0, one launch (start us, length us, event | category | flops | bytes accessed | tf_op | source)
XLA Modules:
  0.0 1666.4 jit_solution(6635196143196874810)
XLA Ops:
  12.3 1.7 convert_element_type.113
  16.0 57.3 %all-gather.12.cloned.1.call-done = bf16[2,768,1024]{2,1,0:T(8,128)(2,1)} async-done(((bf16[2,24,1024]{2,1,0:T(8,128)(2,1)}), bf16[2,768,1024]{2,1,0:T(8,128)(2,1)}) %all-gather.12.cloned.1.call-update) | async-done | bytes 3145744 | tf_op jit(solution)/shard_map/all_gather | solution.py:260
  73.4 3.0 multiply_reduce_fusion.10
  76.4 68.7 %all-gather.16.cloned.1.call-done = bf16[768,4096]{1,0:T(8,128)(2,1)} async-done(((bf16[24,4096]{1,0:T(8,128)(2,1)}), bf16[768,4096]{1,0:T(8,128)(2,1)}) %all-gather.16.cloned.1.call-update) | async-done | bytes 6291472 | tf_op jit(solution)/shard_map/all_gather | solution.py:262
  146.3 55.9 %all-gather.14.cloned.1.call-done = bf16[1001,768]{0,1:T(8,128)(2,1)} async-done(((bf16[1001,24]{0,1:T(8,128)(2,1)}), bf16[1001,768]{0,1:T(8,128)(2,1)}) %all-gather.14.cloned.1.call-update) | async-done | bytes 1537552 | tf_op jit(solution)/shard_map/all_gather | solution.py:261
  202.2 2.0 multiply_reduce_fusion.20
  206.5 3.1 fusion.16
  212.2 36.7 %all-gather.20.cloned.1.call-done = bf16[1024,3,512]{2,0,1:T(8,128)(2,1)} async-done(((bf16[64,3,512]{2,0,1:T(8,128)(2,1)}), bf16[1024,3,512]{2,0,1:T(8,128)(2,1)}) %all-gather.20.cloned.1.call-update) | async-done | bytes 3145744 | tf_op jit(solution)/shard_map/all_gather | solution.py:254
  248.9 33.4 %all-gather.18.cloned.1.call-done = bf16[4,256,1024]{2,1,0:T(8,128)(2,1)} async-done(((bf16[2,256,1024]{2,1,0:T(8,128)(2,1)}), bf16[4,256,1024]{2,1,0:T(8,128)(2,1)}) %all-gather.18.cloned.1.call-update) | async-done | bytes 2097168 | tf_op jit(solution)/shard_map/all_gather | solution.py:86
  282.3 5.9 fusion.29
  290.5 1.9 copy.154
  298.6 24.3 %all-gather.22.cloned.1.call-done = bf16[512,1024]{0,1:T(8,128)(2,1)} async-done(((bf16[512,64]{0,1:T(8,128)(2,1)}), bf16[512,1024]{0,1:T(8,128)(2,1)}) %all-gather.22.cloned.1.call-update) | async-done | bytes 1048592 | tf_op jit(solution)/shard_map/all_gather | solution.py:255
  322.9 4.5 fusion.54
  329.9 50.9 %reduce-scatter.12.cloned.1.call-done = f32[2,256,1024]{2,1,0:T(8,128)} async-done(((f32[4,256,1024]{2,1,0:T(8,128)}), f32[2,256,1024]{2,1,0:T(8,128)}) %reduce-scatter.12.cloned.1.call-update) | async-done | bytes 2097168 | tf_op jit(solution)/shard_map/reduce_scatter | solution.py:90
  380.8 2.5 multiply_reduce_fusion.9
  386.5 59.3 %all-gather.26.cloned.1.call-done = bf16[1024,2,1536]{2,0,1:T(8,128)(2,1)} async-done(((bf16[64,2,1536]{2,0,1:T(8,128)(2,1)}), bf16[1024,2,1536]{2,0,1:T(8,128)(2,1)}) %all-gather.26.cloned.1.call-update) | async-done | bytes 6291472 | tf_op jit(solution)/shard_map/all_gather | solution.py:256
  445.9 33.4 %all-gather.24.cloned.1.call-done = bf16[4,256,1024]{2,1,0:T(8,128)(2,1)} async-done(((bf16[2,256,1024]{2,1,0:T(8,128)(2,1)}), bf16[4,256,1024]{2,1,0:T(8,128)(2,1)}) %all-gather.24.cloned.1.call-update) | async-done | bytes 2097168 | tf_op jit(solution)/shard_map/all_gather | solution.py:86
  479.2 9.4 fusion.9
  488.7 4.6 copy-done.7
  493.2 3.3 multiply_convert_fusion.2
  496.6 31.1 %all-gather.28.cloned.1.call-done = bf16[1536,1024]{0,1:T(8,128)(2,1)} async-done(((bf16[1536,64]{0,1:T(8,128)(2,1)}), bf16[1536,1024]{0,1:T(8,128)(2,1)}) %all-gather.28.cloned.1.call-update) | async-done | bytes 3145744 | tf_op jit(solution)/shard_map/all_gather | solution.py:257
  527.6 8.4 fusion.24
  536.9 52.4 %reduce-scatter.14.cloned.1.call-done = f32[2,256,1024]{2,1,0:T(8,128)} async-done(((f32[4,256,1024]{2,1,0:T(8,128)}), f32[2,256,1024]{2,1,0:T(8,128)}) %reduce-scatter.14.cloned.1.call-update) | async-done | bytes 2097168 | tf_op jit(solution)/shard_map/reduce_scatter | solution.py:90
  589.3 2.0 multiply_reduce_fusion.8
  597.9 33.2 %all-gather.30.cloned.1.call-done = bf16[4,256,1024]{2,1,0:T(8,128)(2,1)} async-done(((bf16[2,256,1024]{2,1,0:T(8,128)(2,1)}), bf16[4,256,1024]{2,1,0:T(8,128)(2,1)}) %all-gather.30.cloned.1.call-update) | async-done | bytes 2097168 | tf_op jit(solution)/shard_map/all_gather | solution.py:86
  631.1 11.2 fusion.28
  645.1 10.2 fusion.32
  655.3 54.4 %reduce-scatter.16.cloned.1.call-done = f32[2,256,1024]{2,1,0:T(8,128)} async-done(((f32[4,256,1024]{2,1,0:T(8,128)}), f32[2,256,1024]{2,1,0:T(8,128)}) %reduce-scatter.16.cloned.1.call-update) | async-done | bytes 2097168 | tf_op jit(solution)/shard_map/reduce_scatter | solution.py:90
  709.7 2.3 multiply_reduce_fusion.3
  712.6 4.2 fusion.115
  717.0 33.0 %all-gather.32.cloned.1.call-done = bf16[4,256,1024]{2,1,0:T(8,128)(2,1)} async-done(((bf16[2,256,1024]{2,1,0:T(8,128)(2,1)}), bf16[4,256,1024]{2,1,0:T(8,128)(2,1)}) %all-gather.32.cloned.1.call-update) | async-done | bytes 2097168 | tf_op jit(solution)/shard_map/all_gather | solution.py:86
  750.1 3.1 convolution_convert_fusion.1
  753.8 5.1 convolution_convert_fusion
  758.9 4.8 multiply_reduce_fusion
  763.7 2.1 multiply_convert_fusion
  772.4 7.6 fusion.35
  780.1 1.8 copy-done.18
  781.9 7.1 convolution_bitcast_fusion.1
  790.2 4.3 convolution_bitcast_fusion.5
  794.5 12.8 convolution_bitcast_fusion
  809.1 7.1 convolution_bitcast_fusion.2
  816.3 18.1 %reduce-scatter.26.cloned.1.call-done = f32[2,256,1024]{2,1,0:T(8,128)} async-done(((f32[4,256,1024]{2,1,0:T(8,128)}), f32[2,256,1024]{2,1,0:T(8,128)}) %reduce-scatter.26.cloned.1.call-update) | async-done | bytes 2097168 | tf_op jit(solution)/shard_map/reduce_scatter | solution.py:90
  834.5 2.1 multiply_reduce_fusion.4
  836.7 6.1 fusion.12
  842.8 2.7 multiply_reduce_fusion.19
  845.5 3.2 fusion.75
  849.2 2.8 convolution_bitcast_fusion.3
  853.1 2.7 convolution_bitcast_fusion.4
  855.9 3.3 pad_maximum_fusion.2
  861.6 3.9 fusion.101
  865.5 5.1 pad_maximum_fusion
  872.1 51.5 %reduce-scatter.24.cloned.1.call-done = f32[1536,64]{0,1:T(8,128)} async-done(((f32[1536,1024]{0,1:T(8,128)}), f32[1536,64]{0,1:T(8,128)}) %reduce-scatter.24.cloned.1.call-update) | async-done | bytes 393232 | tf_op jit(solution)/shard_map/reduce_scatter | solution.py:299
  923.6 1.7 multiply_reduce_fusion.14
  925.3 63.1 %reduce-scatter.20.cloned.1.call-done = f32[512,64]{0,1:T(8,128)} async-done(((f32[512,1024]{0,1:T(8,128)}), f32[512,64]{0,1:T(8,128)}) %reduce-scatter.20.cloned.1.call-update) | async-done | bytes 131088 | tf_op jit(solution)/shard_map/reduce_scatter | solution.py:297
  989.9 136.0 %reduce-scatter.22.cloned.1.call-done = f32[64,2,1536]{2,0,1:T(8,128)} async-done(((f32[1024,2,1536]{2,0,1:T(8,128)}), f32[64,2,1536]{2,0,1:T(8,128)}) %reduce-scatter.22.cloned.1.call-update) | async-done | bytes 786448 | tf_op jit(solution)/shard_map/reduce_scatter | solution.py:298
  1125.9 1.9 multiply_reduce_fusion.12
  1127.9 86.4 %reduce-scatter.18.cloned.1.call-done = f32[64,3,512]{2,0,1:T(8,128)} async-done(((f32[1024,3,512]{2,0,1:T(8,128)}), f32[64,3,512]{2,0,1:T(8,128)}) %reduce-scatter.18.cloned.1.call-update) | async-done | bytes 393232 | tf_op jit(solution)/shard_map/reduce_scatter | solution.py:296
  1214.3 1.7 multiply_reduce_fusion.15
  1218.6 102.8 %reduce-scatter.30.cloned.1.call-done = f32[1001,24]{0,1:T(8,128)} async-done(((f32[1001,768]{0,1:T(8,128)}), f32[1001,24]{0,1:T(8,128)}) %reduce-scatter.30.cloned.1.call-update) | async-done | bytes 96112 | tf_op jit(solution)/shard_map/reduce_scatter | solution.py:312
  1322.9 118.4 %reduce-scatter.28.cloned.1.call-done = f32[2,24,1024]{2,1,0:T(8,128)} async-done(((f32[2,768,1024]{2,1,0:T(8,128)}), f32[2,24,1024]{2,1,0:T(8,128)}) %reduce-scatter.28.cloned.1.call-update) | async-done | bytes 196624 | tf_op jit(solution)/shard_map/reduce_scatter | solution.py:311
  1444.1 158.1 %reduce-scatter.32.cloned.1.call-done = f32[24,4096]{1,0:T(8,128)} async-done(((f32[768,4096]{1,0:T(8,128)}), f32[24,4096]{1,0:T(8,128)}) %reduce-scatter.32.cloned.1.call-update) | async-done | bytes 393232 | tf_op jit(solution)/shard_map/reduce_scatter | solution.py:313
  1602.2 1.7 multiply_reduce_fusion.13
  1604.6 40.2 %all-reduce = (f32[]{:T(128)}, f32[]{:T(128)}) all-reduce(f32[]{:T(128)} %multiply_reduce_fusion.21, f32[]{:T(128)S(6)} %add.296), channel_id=1, replica_groups=mesh['dp'=16,'tensor'=2] {'dp','tensor'}, use_global_device_ids=true, to_apply=%region_11.12 | all-reduce | flops 2 | bytes 16 | tf_op jit(solution)/shard_map/psum | solution.py:281
  1645.6 1.8 multiply_subtract_fusion
  (295 shorter events, 68.3 us)
Async XLA Ops:
  7.2 66.2 %all-gather.12.cloned.1.call-start = ((), (), s32[]{:S(2)}) async-start(), calls=%async_computation.11 | async-start | bytes 3244032 | tf_op jit(solution)/shard_map/all_gather | solution.py:260
  8.8 136.3 %all-gather.16.cloned.1.call-start = ((), (), s32[]{:S(2)}) async-start(), calls=%async_computation.13 | async-start | bytes 6488064 | tf_op jit(solution)/shard_map/all_gather | solution.py:262
  10.6 191.6 %all-gather.14.cloned.1.call-start = ((), (), s32[]{:S(2)}) async-start(), calls=%async_computation.12 | async-start | bytes 1622016 | tf_op jit(solution)/shard_map/all_gather | solution.py:261
  12.2 236.7 %all-gather.20.cloned.1.call-start = ((), (), s32[]{:S(2)}) async-start(), calls=%async_computation.15 | async-start | bytes 3342336 | tf_op jit(solution)/shard_map/all_gather | solution.py:254
  14.0 268.3 %all-gather.18.cloned.1.call-start = ((), (), s32[]{:S(2)}) async-start(), calls=%async_computation.14 | async-start | bytes 3145728 | tf_op jit(solution)/shard_map/all_gather | solution.py:86
  14.7 187.5 %copy-start.76 = (s32[2]{0:T(128)}, s32[2]{0:T(128)S(1)}, u32[]{:S(2)}) copy-start(s32[2]{0:T(128)S(1)} %compare_select_fusion) | copy-start | bytes 28
  15.9 60.5 %copy-start.80 = (f32[2]{0:T(128)}, f32[2]{0:T(128)S(1)}, u32[]{:S(2)}) copy-start(f32[2]{0:T(128)S(1)} %get-tuple-element.153) | copy-start | bytes 28
  15.9 60.5 %copy-start.82 = (f32[2]{0:T(128)}, f32[2]{0:T(128)S(1)}, u32[]{:S(2)}) copy-start(f32[2]{0:T(128)S(1)} %get-tuple-element.165) | copy-start | bytes 28
  16.0 129.1 %copy-start.72 = (bf16[2,128]{1,0:T(2,128)(2,1)}, bf16[2,128]{1,0:T(2,128)(2,1)S(1)}, u32[]{:S(2)}) copy-start(bf16[2,128]{1,0:T(2,128)(2,1)S(1)} %get-tuple-element.162) | copy-start | bytes 1540
  16.0 129.1 %copy-start.74 = (bf16[2,128]{1,0:T(2,128)(2,1)}, bf16[2,128]{1,0:T(2,128)(2,1)S(1)}, u32[]{:S(2)}) copy-start(bf16[2,128]{1,0:T(2,128)(2,1)S(1)} %get-tuple-element.163) | copy-start | bytes 1540
  76.4 68.7 %copy-start.68 = (f32[2,256]{1,0:T(2,128)}, f32[2,256]{1,0:T(2,128)S(1)}, u32[]{:S(2)}) copy-start(f32[2,256]{1,0:T(2,128)S(1)} %get-tuple-element.168) | copy-start | bytes 6148
  76.4 133.8 %copy-start.4 = (f32[2,256,1024]{2,1,0:T(8,128)}, f32[2,256,1024]{2,1,0:T(8,128)S(1)}, u32[]{:S(2)}) copy-start(f32[2,256,1024]{2,1,0:T(8,128)S(1)} %get-tuple-element.169) | copy-start | bytes 6291460
  76.4 133.8 %copy-start.64 = (f32[2,256]{1,0:T(2,128)}, f32[2,256]{1,0:T(2,128)S(1)}, u32[]{:S(2)}) copy-start(f32[2,256]{1,0:T(2,128)S(1)} %fusion.85) | copy-start | bytes 6148
  211.5 111.4 %all-gather.22.cloned.1.call-start = ((), (), s32[]{:S(2)}) async-start(), calls=%async_computation.16 | async-start | bytes 1114112 | tf_op jit(solution)/shard_map/all_gather | solution.py:255
  212.2 168.6 %reduce-scatter.12.cloned.1.call-start = ((), (), s32[]{:S(2)}) async-start(), calls=%async_computation.17 | async-start | bytes 6291456 | tf_op jit(solution)/shard_map/reduce_scatter | solution.py:90
  298.6 28.8 %copy-start.14 = (bf16[4,8,64,256]{3,2,1,0:T(8,128)(2,1)}, bf16[4,8,64,256]{3,2,1,0:T(8,128)(2,1)S(1)}, u32[]{:S(2)}) copy-start(bf16[4,8,64,256]{3,2,1,0:T(8,128)(2,1)S(1)} %convolution_convert_fusion.2) | copy-start | bytes 3145732
  327.4 118.5 %all-gather.26.cloned.1.call-start = ((), (), s32[]{:S(2)}) async-start(), calls=%async_computation.19 | async-start | bytes 6684672 | tf_op jit(solution)/shard_map/all_gather | solution.py:256
  329.4 149.8 %all-gather.24.cloned.1.call-start = ((), (), s32[]{:S(2)}) async-start(), calls=%async_computation.18 | async-start | bytes 3145728 | tf_op jit(solution)/shard_map/all_gather | solution.py:86
  385.7 141.9 %all-gather.28.cloned.1.call-start = ((), (), s32[]{:S(2)}) async-start(), calls=%async_computation.20 | async-start | bytes 3342336 | tf_op jit(solution)/shard_map/all_gather | solution.py:257
  386.5 202.8 %reduce-scatter.14.cloned.1.call-start = ((), (), s32[]{:S(2)}) async-start(), calls=%async_computation.21 | async-start | bytes 6291456 | tf_op jit(solution)/shard_map/reduce_scatter | solution.py:90
  488.6 4.6 copy-start.7
  536.0 95.1 %all-gather.30.cloned.1.call-start = ((), (), s32[]{:S(2)}) async-start(), calls=%async_computation.22 | async-start | bytes 3145728 | tf_op jit(solution)/shard_map/all_gather | solution.py:86
  536.9 54.5 %copy-start.83 = (f32[2]{0:T(128)S(1)}, f32[2]{0:T(128)}, u32[]{:S(2)}) copy-start(f32[2]{0:T(128)} %copy-done.82) | copy-start | bytes 28
  536.9 54.5 %copy-start.84 = (f32[2]{0:T(128)S(1)}, f32[2]{0:T(128)}, u32[]{:S(2)}) copy-start(f32[2]{0:T(128)} %get-tuple-element.152) | copy-start | bytes 28
  597.8 111.9 %reduce-scatter.16.cloned.1.call-start = ((), (), s32[]{:S(2)}) async-start(), calls=%async_computation.23 | async-start | bytes 6291456 | tf_op jit(solution)/shard_map/reduce_scatter | solution.py:90
  655.3 54.5 %copy-start.62 = (f32[2,256]{1,0:T(2,128)S(1)}, f32[2,256]{1,0:T(2,128)}, u32[]{:S(2)}) copy-start(f32[2,256]{1,0:T(2,128)} %copy-done.61) | copy-start | bytes 6148
  655.3 56.7 %copy-start.67 = (f32[2,256]{1,0:T(2,128)S(1)}, f32[2,256]{1,0:T(2,128)}, u32[]{:S(2)}) copy-start(f32[2,256]{1,0:T(2,128)} %copy-done.66) | copy-start | bytes 6148
  655.3 94.8 %all-gather.32.cloned.1.call-start = ((), (), s32[]{:S(2)}) async-start(), calls=%async_computation.24 | async-start | bytes 3145728 | tf_op jit(solution)/shard_map/all_gather | solution.py:86
  716.8 36.9 %copy-start.35 = (f32[4,8,256]{2,1,0:T(8,128)S(1)}, f32[4,8,256]{2,1,0:T(8,128)}, u32[]{:S(2)}) copy-start(f32[4,8,256]{2,1,0:T(8,128)} %copy-done.34) | copy-start | bytes 98308
  716.8 117.6 %reduce-scatter.26.cloned.1.call-start = ((), (), s32[]{:S(2)}) async-start(), calls=%async_computation.29 | async-start | bytes 6291456 | tf_op jit(solution)/shard_map/reduce_scatter | solution.py:90
  753.7 9.9 slice-start
  758.9 4.8 slice-start.1
  780.0 143.6 %reduce-scatter.24.cloned.1.call-start = ((), (), s32[]{:S(2)}) async-start(), calls=%async_computation.28 | async-start | bytes 6684672 | tf_op jit(solution)/shard_map/reduce_scatter | solution.py:299
  789.0 5.5 copy-start.86
  789.0 199.4 %reduce-scatter.20.cloned.1.call-start = ((), (), s32[]{:S(2)}) async-start(), calls=%async_computation.26 | async-start | bytes 2228224 | tf_op jit(solution)/shard_map/reduce_scatter | solution.py:297
  794.5 331.5 %reduce-scatter.22.cloned.1.call-start = ((), (), s32[]{:S(2)}) async-start(), calls=%async_computation.27 | async-start | bytes 13369344 | tf_op jit(solution)/shard_map/reduce_scatter | solution.py:298
  807.3 407.0 %reduce-scatter.18.cloned.1.call-start = ((), (), s32[]{:S(2)}) async-start(), calls=%async_computation.25 | async-start | bytes 6684672 | tf_op jit(solution)/shard_map/reduce_scatter | solution.py:296
  816.3 18.2 %copy-start.5 = (f32[2,256,1024]{2,1,0:T(8,128)S(1)}, f32[2,256,1024]{2,1,0:T(8,128)}, u32[]{:S(2)}) copy-start(f32[2,256,1024]{2,1,0:T(8,128)} %copy-done.4) | copy-start | bytes 6291460
  816.3 18.2 %copy-start.65 = (f32[2,256]{1,0:T(2,128)S(1)}, f32[2,256]{1,0:T(2,128)}, u32[]{:S(2)}) copy-start(f32[2,256]{1,0:T(2,128)} %copy-done.64) | copy-start | bytes 6148
  816.3 505.1 %reduce-scatter.30.cloned.1.call-start = ((), (), s32[]{:S(2)}) async-start(), calls=%async_computation.31 | async-start | bytes 3244032 | tf_op jit(solution)/shard_map/reduce_scatter | solution.py:312
  836.6 6.2 copy-start.52
  836.6 6.2 copy-start.56
  836.6 8.8 copy-start.79
  836.6 8.8 copy-start.71
  836.6 8.8 copy-start.77
  848.7 592.5 %reduce-scatter.28.cloned.1.call-start = ((), (), s32[]{:S(2)}) async-start(), calls=%async_computation.30 | async-start | bytes 6488064 | tf_op jit(solution)/shard_map/reduce_scatter | solution.py:311
  849.2 3.9 copy-start.20
  859.2 743.1 %reduce-scatter.32.cloned.1.call-start = ((), (), s32[]{:S(2)}) async-start(), calls=%async_computation.32 | async-start | bytes 12976128 | tf_op jit(solution)/shard_map/reduce_scatter | solution.py:313
  870.6 774.9 %copy-start.17 = (f32[64,2,1536]{2,1,0:T(2,128)S(1)}, f32[64,2,1536]{2,1,0:T(2,128)}, u32[]{:S(2)}) copy-start(f32[64,2,1536]{2,1,0:T(2,128)} %param.41) | copy-start | bytes 2359300
  870.6 774.9 %copy-start.38 = (f32[64,2,1536]{2,1,0:T(2,128)S(1)}, f32[64,2,1536]{2,1,0:T(2,128)}, u32[]{:S(2)}) copy-start(f32[64,2,1536]{2,1,0:T(2,128)} %param.43) | copy-start | bytes 2359300
  870.6 775.0 %copy-start.39 = (f32[64,2,1536]{2,1,0:T(2,128)S(1)}, f32[64,2,1536]{2,1,0:T(2,128)}, u32[]{:S(2)}) copy-start(f32[64,2,1536]{2,1,0:T(2,128)} %param.42) | copy-start | bytes 2359300
  1647.4 4.6 copy-start.21
  1647.4 4.6 copy-start.26
  1647.4 4.6 copy-start.43
  1647.4 4.5 copy-start.44
  1648.9 4.3 copy-start.41
  1648.9 4.3 copy-start.42
  1648.9 4.3 copy-start.57
  1648.9 4.3 copy-start.58
  1648.9 5.2 copy-start.23
  1648.9 5.2 copy-start.25
  1649.0 5.2 copy-start.45
  1649.0 5.2 copy-start.46
  1653.3 3.8 copy-start.24
  (53 other events, 122.0 us)
Sparse Core Ops, SparseCore 0:
  11.5 61.7 all-gather.11
  76.8 68.2 all-gather.15
  148.6 53.5 all-gather.13
  204.8 44.0 all-gather.19
  250.3 31.9 all-gather.17
  284.9 37.9 all-gather.21
  327.5 53.2 reduce-scatter.11
  383.9 61.9 all-gather.25
  447.5 31.6 all-gather.23
  482.2 45.4 all-gather.27
  536.2 53.0 reduce-scatter.13
  597.9 33.1 all-gather.29
  655.4 54.2 reduce-scatter.15
  716.9 33.1 all-gather.31
  780.1 54.2 reduce-scatter.25
  838.2 85.3 reduce-scatter.23
  927.7 60.6 reduce-scatter.19
  992.3 133.5 reduce-scatter.21
  1129.9 84.3 reduce-scatter.17
  1220.4 100.8 reduce-scatter.29
  1327.9 113.2 reduce-scatter.27
  1447.3 154.9 reduce-scatter.31
where the time goes:
time: 1680 us; the launch traced here: 1670 us
  waiting for transfers between devices  1360 us (81%)
  matrix products  143 us (9%)
  other arithmetic  62.7 us (4%)
  blocking collectives  40.2 us (2%)
  local copies, waits for them, and re-layouts  36.4 us (2%)
  between operations  23 us (1%)
    reduce_scatter x4, waiting for transfers between devices, pair_sum(): return lax.psum_scatter(value, 'tensor', scatter_dimension=0, tiled=True)  176 us
    reduce_scatter x1, waiting for transfers between devices, body(): lax.psum_scatter(mapping_grad, ('dp', 'tensor'), scatter_dimension=0, til...  158 us
    reduce_scatter x1, waiting for transfers between devices, body(): lax.psum_scatter(big_grads[2], 'dp', scatter_dimension=0, tiled=True)  136 us
    all_gather x4, waiting for transfers between devices, pair_rows(): return lax.all_gather(value, 'tensor', axis=0, tiled=True)  133 us
    reduce_scatter x1, waiting for transfers between devices, body(): lax.psum_scatter(patch_grads, ('dp', 'tensor'), scatter_dimension=1, tile...  118 us
    dot_general x23, matrix products, einsum_low(): return jnp.einsum(form, left, right, preferred_element_type=jnp.float32)  118 us
    reduce_scatter x1, waiting for transfers between devices, body(): lax.psum_scatter(table_grad, ('dp', 'tensor'), scatter_dimension=1, tiled...  103 us
    reduce_scatter x1, waiting for transfers between devices, body(): lax.psum_scatter(big_grads[0], 'dp', scatter_dimension=0, tiled=True)  86.4 us
  transfers between devices with their start and end apart: 22, of which 22 were waited for; matrix products, arithmetic and copies ran while one was open for 8% of the time, Pallas kernels for 0%

commit v1 on v0

--- a/solution.py
+++ b/solution.py
@@ -22,6 +22,27 @@
 ADAM_EPS = 1e-08
 CLIP = 0.02
 NORM_EPS = 1e-06
+
+
+def ring_gather(shard, axis, dim):
+    size, place, rows = (lax.axis_size(axis), lax.axis_index(axis), shard.shape[dim])
+    forward = [(i, (i + 1) % size) for i in range(size)]
+    behind = [(i, (i - 1) % size) for i in range(size)]
+    out = jnp.zeros((*shard.shape[:dim], size * rows, *shard.shape[dim + 1 :]), shard.dtype)
+    out = lax.dynamic_update_slice_in_dim(out, shard, place * rows, axis=dim)
+    from_left = from_right = shard
+    half = size // 2
+    for step in range(1, half + 1):
+        from_left = lax.ppermute(from_left, axis, forward)
+        out = lax.dynamic_update_slice_in_dim(
+            out, from_left, (place - step) % size * rows, axis=dim
+        )
+        if step < size - half:
+            from_right = lax.ppermute(from_right, axis, behind)
+            out = lax.dynamic_update_slice_in_dim(
+                out, from_right, (place + step) % size * rows, axis=dim
+            )
+    return out
 
 
 def to_low(value):
@@ -251,7 +272,7 @@
         second_mapping,
     )
     big = (
-        lax.all_gather(inward.astype(jnp.bfloat16), "dp", axis=0, tiled=True),
+        ring_gather(inward.astype(jnp.bfloat16), "dp", 0),
         lax.all_gather(outward.astype(jnp.bfloat16), "dp", axis=1, tiled=True),
         lax.all_gather(expand.astype(jnp.bfloat16), "dp", axis=0, tiled=True),
         lax.all_gather(shrink.astype(jnp.bfloat16), "dp", axis=1, tiled=True),

time: 1680 us -> 1670 us (level)
  waiting for transfers between devices: 1360 us -> 1320 us
  starting transfers between devices: 2.17 us -> 34.3 us
    all_gather x4, waiting for transfers between devices: 133 us -> 98.5 us  [pair_rows(): return lax.all_gather(value, 'tensor', axis=0, tiled=True)]
    ppermute x0 -> x15, starting transfers between devices: none -> 31.7 us  [the longest x7 31.1 us: ring_gather(): from_right = lax.ppermute(from_right, axis, behind)]
    ppermute x0 -> x15, waiting for transfers between devices: none -> 30.7 us  [the longest x8 30.7 us: ring_gather(): from_left = lax.ppermute(from_left, axis, forward)]
    all_gather x1, waiting for transfers between devices: 24.3 us -> 0.02 us  [body(): lax.all_gather(outward.astype(jnp.bfloat16), 'dp', axis=1, tiled=True)]
  transfers between devices with their start and end apart: 22 -> 37, of which waited for: 22 -> 28; matrix products, arithmetic and copies ran while one was open for 8% -> 9% of each run, Pallas kernels for 0% -> 0%
where the time goes in v1:
time: 1670 us; the launch traced here: 1660 us
  waiting for transfers between devices  1320 us (79%)
  matrix products  145 us (9%)
  other arithmetic  65.2 us (4%)
  blocking collectives  40.2 us (2%)
  local copies, waits for them, and re-layouts  35.4 us (2%)
  starting transfers between devices  34.3 us (2%)
  between operations  23.3 us (1%)
    reduce_scatter x4, waiting for transfers between devices, pair_sum(): return lax.psum_scatter(value, 'tensor', scatter_dimension=0, tiled=True)  174 us
    reduce_scatter x1, waiting for transfers between devices, body(): lax.psum_scatter(mapping_grad, ('dp', 'tensor'), scatter_dimension=0, til...  158 us
    reduce_scatter x1, waiting for transfers between devices, body(): lax.psum_scatter(big_grads[2], 'dp', scatter_dimension=0, tiled=True)  136 us
    dot_general x23, matrix products, einsum_low(): return jnp.einsum(form, left, right, preferred_element_type=jnp.float32)  119 us
    reduce_scatter x1, waiting for transfers between devices, body(): lax.psum_scatter(patch_grads, ('dp', 'tensor'), scatter_dimension=1, tile...  118 us
    reduce_scatter x1, waiting for transfers between devices, body(): lax.psum_scatter(table_grad, ('dp', 'tensor'), scatter_dimension=1, tiled...  103 us
    all_gather x4, waiting for transfers between devices, pair_rows(): return lax.all_gather(value, 'tensor', axis=0, tiled=True)  98.5 us
    reduce_scatter x1, waiting for transfers between devices, body(): lax.psum_scatter(big_grads[0], 'dp', scatter_dimension=0, tiled=True)  86.4 us
  transfers between devices with their start and end apart: 37, of which 28 were waited for; matrix products, arithmetic and copies ran while one was open for 9% of the time, Pallas kernels for 0%

profile of v1, /device:TPU:0, one launch (start us, length us, event | category | flops | bytes accessed | tf_op | source)
XLA Modules:
  0.0 1659.6 jit_solution(10706130411443486422)
XLA Ops:
  14.3 59.1 %all-gather.12.cloned.1.call-done = bf16[2,768,1024]{2,1,0:T(8,128)(2,1)} async-done(((bf16[2,24,1024]{2,1,0:T(8,128)(2,1)}), bf16[2,768,1024]{2,1,0:T(8,128)(2,1)}) %all-gather.12.cloned.1.call-update) | async-done | bytes 3145744 | tf_op jit(solution)/shard_map/all_gather | solution.py:281
  73.4 3.0 multiply_reduce_fusion.10
  76.4 68.7 %all-gather.16.cloned.1.call-done = bf16[768,4096]{1,0:T(8,128)(2,1)} async-done(((bf16[24,4096]{1,0:T(8,128)(2,1)}), bf16[768,4096]{1,0:T(8,128)(2,1)}) %all-gather.16.cloned.1.call-update) | async-done | bytes 6291472 | tf_op jit(solution)/shard_map/all_gather | solution.py:283
  146.3 55.9 %all-gather.14.cloned.1.call-done = bf16[1001,768]{0,1:T(8,128)(2,1)} async-done(((bf16[1001,24]{0,1:T(8,128)(2,1)}), bf16[1001,768]{0,1:T(8,128)(2,1)}) %all-gather.14.cloned.1.call-update) | async-done | bytes 1537552 | tf_op jit(solution)/shard_map/all_gather | solution.py:282
  206.5 3.1 fusion.16
  212.8 4.2 collective-permute-start.1
  220.6 4.4 collective-permute-start.3
  225.1 3.4 collective-permute-done.2
  228.5 4.4 collective-permute-start.5
  233.0 3.4 collective-permute-done.4
  236.4 4.4 collective-permute-start.7
  240.9 3.4 collective-permute-done.6
  244.3 4.4 collective-permute-start.9
  248.8 3.3 collective-permute-done.8
  252.1 4.5 collective-permute-start.11
  256.7 3.8 collective-permute-done.10
  260.5 4.6 collective-permute-start.13
  265.2 3.5 collective-permute-done.12
  269.0 8.2 collective-permute-done.14
  277.2 5.2 fusion.29
  292.9 4.9 fusion.54
  299.9 49.5 %reduce-scatter.12.cloned.1.call-done = f32[2,256,1024]{2,1,0:T(8,128)} async-done(((f32[4,256,1024]{2,1,0:T(8,128)}), f32[2,256,1024]{2,1,0:T(8,128)}) %reduce-scatter.12.cloned.1.call-update) | async-done | bytes 2097168 | tf_op jit(solution)/shard_map/reduce_scatter | solution.py:111
  354.4 60.1 %all-gather.24.cloned.1.call-done = bf16[1024,2,1536]{2,0,1:T(8,128)(2,1)} async-done(((bf16[64,2,1536]{2,0,1:T(8,128)(2,1)}), bf16[1024,2,1536]{2,0,1:T(8,128)(2,1)}) %all-gather.24.cloned.1.call-update) | async-done | bytes 6291472 | tf_op jit(solution)/shard_map/all_gather | solution.py:277
  414.5 33.4 %all-gather.22.cloned.1.call-done = bf16[4,256,1024]{2,1,0:T(8,128)(2,1)} async-done(((bf16[2,256,1024]{2,1,0:T(8,128)(2,1)}), bf16[4,256,1024]{2,1,0:T(8,128)(2,1)}) %all-gather.22.cloned.1.call-update) | async-done | bytes 2097168 | tf_op jit(solution)/shard_map/all_gather | solution.py:107
  447.9 9.4 fusion.9
  457.3 4.6 copy-done.8
  461.9 3.4 multiply_convert_fusion.2
  465.3 30.9 %all-gather.26.cloned.1.call-done = bf16[1536,1024]{0,1:T(8,128)(2,1)} async-done(((bf16[1536,64]{0,1:T(8,128)(2,1)}), bf16[1536,1024]{0,1:T(8,128)(2,1)}) %all-gather.26.cloned.1.call-update) | async-done | bytes 3145744 | tf_op jit(solution)/shard_map/all_gather | solution.py:278
  496.2 8.3 fusion.24
  505.4 52.4 %reduce-scatter.14.cloned.1.call-done = f32[2,256,1024]{2,1,0:T(8,128)} async-done(((f32[4,256,1024]{2,1,0:T(8,128)}), f32[2,256,1024]{2,1,0:T(8,128)}) %reduce-scatter.14.cloned.1.call-update) | async-done | bytes 2097168 | tf_op jit(solution)/shard_map/reduce_scatter | solution.py:111
  566.9 32.6 %all-gather.28.cloned.1.call-done = bf16[4,256,1024]{2,1,0:T(8,128)(2,1)} async-done(((bf16[2,256,1024]{2,1,0:T(8,128)(2,1)}), bf16[4,256,1024]{2,1,0:T(8,128)(2,1)}) %all-gather.28.cloned.1.call-update) | async-done | bytes 2097168 | tf_op jit(solution)/shard_map/all_gather | solution.py:107
  599.5 11.3 fusion.28
  613.4 10.1 fusion.32
  623.6 54.4 %reduce-scatter.16.cloned.1.call-done = f32[2,256,1024]{2,1,0:T(8,128)} async-done(((f32[4,256,1024]{2,1,0:T(8,128)}), f32[2,256,1024]{2,1,0:T(8,128)}) %reduce-scatter.16.cloned.1.call-update) | async-done | bytes 2097168 | tf_op jit(solution)/shard_map/reduce_scatter | solution.py:111
  680.9 4.2 fusion.115
  685.9 32.5 %all-gather.30.cloned.1.call-done = bf16[4,256,1024]{2,1,0:T(8,128)(2,1)} async-done(((bf16[2,256,1024]{2,1,0:T(8,128)(2,1)}), bf16[4,256,1024]{2,1,0:T(8,128)(2,1)}) %all-gather.30.cloned.1.call-update) | async-done | bytes 2097168 | tf_op jit(solution)/shard_map/all_gather | solution.py:107
  718.4 3.1 convolution_convert_fusion.1
  722.0 4.9 convolution_convert_fusion
  728.3 4.8 multiply_reduce_fusion
  733.1 4.6 multiply_convert_fusion
  741.0 3.1 multiply_convert_fusion.4
  744.7 22.0 %all-gather.32.cloned.1.call-done = bf16[1024,3,512]{2,0,1:T(8,128)(2,1)} async-done(((bf16[64,3,512]{2,0,1:T(8,128)(2,1)}), bf16[1024,3,512]{2,0,1:T(8,128)(2,1)}) %all-gather.32.cloned.1.call-update) | async-done | bytes 3145744 | tf_op jit(solution)/shard_map/all_gather | solution.py:305
  766.7 7.6 fusion.35
  776.2 7.0 convolution_bitcast_fusion.1
  784.5 4.3 convolution_bitcast_fusion.5
  788.8 12.6 convolution_bitcast_fusion
  803.2 7.1 convolution_bitcast_fusion.2
  810.4 17.2 %reduce-scatter.26.cloned.1.call-done = f32[2,256,1024]{2,1,0:T(8,128)} async-done(((f32[4,256,1024]{2,1,0:T(8,128)}), f32[2,256,1024]{2,1,0:T(8,128)}) %reduce-scatter.26.cloned.1.call-update) | async-done | bytes 2097168 | tf_op jit(solution)/shard_map/reduce_scatter | solution.py:111
  829.8 6.1 fusion.12
  835.9 2.7 multiply_reduce_fusion.19
  838.6 3.2 fusion.75
  842.4 2.8 convolution_bitcast_fusion.3
  846.3 2.7 convolution_bitcast_fusion.4
  849.0 3.3 pad_maximum_fusion.2
  854.8 3.9 fusion.101
  858.7 5.1 pad_maximum_fusion
  865.3 51.4 %reduce-scatter.24.cloned.1.call-done = f32[1536,64]{0,1:T(8,128)} async-done(((f32[1536,1024]{0,1:T(8,128)}), f32[1536,64]{0,1:T(8,128)}) %reduce-scatter.24.cloned.1.call-update) | async-done | bytes 393232 | tf_op jit(solution)/shard_map/reduce_scatter | solution.py:320
  918.4 63.2 %reduce-scatter.20.cloned.1.call-done = f32[512,64]{0,1:T(8,128)} async-done(((f32[512,1024]{0,1:T(8,128)}), f32[512,64]{0,1:T(8,128)}) %reduce-scatter.20.cloned.1.call-update) | async-done | bytes 131088 | tf_op jit(solution)/shard_map/reduce_scatter | solution.py:318
  983.2 136.1 %reduce-scatter.22.cloned.1.call-done = f32[64,2,1536]{2,0,1:T(8,128)} async-done(((f32[1024,2,1536]{2,0,1:T(8,128)}), f32[64,2,1536]{2,0,1:T(8,128)}) %reduce-scatter.22.cloned.1.call-update) | async-done | bytes 786448 | tf_op jit(solution)/shard_map/reduce_scatter | solution.py:319
  1121.2 86.4 %reduce-scatter.18.cloned.1.call-done = f32[64,3,512]{2,0,1:T(8,128)} async-done(((f32[1024,3,512]{2,0,1:T(8,128)}), f32[64,3,512]{2,0,1:T(8,128)}) %reduce-scatter.18.cloned.1.call-update) | async-done | bytes 393232 | tf_op jit(solution)/shard_map/reduce_scatter | solution.py:317
  1211.9 102.7 %reduce-scatter.30.cloned.1.call-done = f32[1001,24]{0,1:T(8,128)} async-done(((f32[1001,768]{0,1:T(8,128)}), f32[1001,24]{0,1:T(8,128)}) %reduce-scatter.30.cloned.1.call-update) | async-done | bytes 96112 | tf_op jit(solution)/shard_map/reduce_scatter | solution.py:333
  1316.1 118.3 %reduce-scatter.28.cloned.1.call-done = f32[2,24,1024]{2,1,0:T(8,128)} async-done(((f32[2,768,1024]{2,1,0:T(8,128)}), f32[2,24,1024]{2,1,0:T(8,128)}) %reduce-scatter.28.cloned.1.call-update) | async-done | bytes 196624 | tf_op jit(solution)/shard_map/reduce_scatter | solution.py:332
  1437.3 158.1 %reduce-scatter.32.cloned.1.call-done = f32[24,4096]{1,0:T(8,128)} async-done(((f32[768,4096]{1,0:T(8,128)}), f32[24,4096]{1,0:T(8,128)}) %reduce-scatter.32.cloned.1.call-update) | async-done | bytes 393232 | tf_op jit(solution)/shard_map/reduce_scatter | solution.py:334
  1597.7 40.2 %all-reduce = (f32[]{:T(128)}, f32[]{:T(128)}) all-reduce(f32[]{:T(128)} %multiply_reduce_fusion.21, f32[]{:T(128)S(6)} %add.457), channel_id=1, replica_groups=mesh['dp'=16,'tensor'=2] {'dp','tensor'}, use_global_device_ids=true, to_apply=%region_11.12 | all-reduce | flops 2 | bytes 16 | tf_op jit(solution)/shard_map/psum | solution.py:302
  (334 shorter events, 94.9 us)
Async XLA Ops:
  7.2 66.2 %all-gather.12.cloned.1.call-start = ((), (), s32[]{:S(2)}) async-start(), calls=%async_computation.11 | async-start | bytes 3244032 | tf_op jit(solution)/shard_map/all_gather | solution.py:281
  8.8 136.3 %all-gather.16.cloned.1.call-start = ((), (), s32[]{:S(2)}) async-start(), calls=%async_computation.13 | async-start | bytes 6488064 | tf_op jit(solution)/shard_map/all_gather | solution.py:283
  10.6 191.6 %all-gather.14.cloned.1.call-start = ((), (), s32[]{:S(2)}) async-start(), calls=%async_computation.12 | async-start | bytes 1622016 | tf_op jit(solution)/shard_map/all_gather | solution.py:282
  12.2 265.0 %all-gather.18.cloned.1.call-start = ((), (), s32[]{:S(2)}) async-start(), calls=%async_computation.14 | async-start | bytes 3145728 | tf_op jit(solution)/shard_map/all_gather | solution.py:107
  12.9 189.2 %copy-start.75 = (s32[2]{0:T(128)}, s32[2]{0:T(128)S(1)}, u32[]{:S(2)}) copy-start(s32[2]{0:T(128)S(1)} %compare_select_fusion) | copy-start | bytes 28
  14.1 62.2 %copy-start.79 = (f32[2]{0:T(128)}, f32[2]{0:T(128)S(1)}, u32[]{:S(2)}) copy-start(f32[2]{0:T(128)S(1)} %get-tuple-element.155) | copy-start | bytes 28
  14.1 62.2 %copy-start.81 = (f32[2]{0:T(128)}, f32[2]{0:T(128)S(1)}, u32[]{:S(2)}) copy-start(f32[2]{0:T(128)S(1)} %get-tuple-element.167) | copy-start | bytes 28
  14.3 130.9 %copy-start.71 = (bf16[2,128]{1,0:T(2,128)(2,1)}, bf16[2,128]{1,0:T(2,128)(2,1)S(1)}, u32[]{:S(2)}) copy-start(bf16[2,128]{1,0:T(2,128)(2,1)S(1)} %get-tuple-element.164) | copy-start | bytes 1540
  14.3 130.8 %copy-start.73 = (bf16[2,128]{1,0:T(2,128)(2,1)}, bf16[2,128]{1,0:T(2,128)(2,1)S(1)}, u32[]{:S(2)}) copy-start(bf16[2,128]{1,0:T(2,128)(2,1)S(1)} %get-tuple-element.165) | copy-start | bytes 1540
  76.4 68.7 %copy-start.67 = (f32[2,256]{1,0:T(2,128)}, f32[2,256]{1,0:T(2,128)S(1)}, u32[]{:S(2)}) copy-start(f32[2,256]{1,0:T(2,128)S(1)} %get-tuple-element.170) | copy-start | bytes 6148
  76.4 133.8 %copy-start.5 = (f32[2,256,1024]{2,1,0:T(8,128)}, f32[2,256,1024]{2,1,0:T(8,128)S(1)}, u32[]{:S(2)}) copy-start(f32[2,256,1024]{2,1,0:T(8,128)S(1)} %get-tuple-element.171) | copy-start | bytes 6291460
  76.4 133.8 %copy-start.65 = (f32[2,256]{1,0:T(2,128)}, f32[2,256]{1,0:T(2,128)S(1)}, u32[]{:S(2)}) copy-start(f32[2,256]{1,0:T(2,128)S(1)} %fusion.85) | copy-start | bytes 6148
  211.5 81.5 %all-gather.20.cloned.1.call-start = ((), (), s32[]{:S(2)}) async-start(), calls=%async_computation.15 | async-start | bytes 1114112 | tf_op jit(solution)/shard_map/all_gather | solution.py:276
  212.5 8.1 collective-permute-start
  212.8 7.8 collective-permute-start.1
  218.5 130.9 %reduce-scatter.12.cloned.1.call-start = ((), (), s32[]{:S(2)}) async-start(), calls=%async_computation.16 | async-start | bytes 6291456 | tf_op jit(solution)/shard_map/reduce_scatter | solution.py:111
  220.6 7.9 collective-permute-start.2
  220.6 7.9 collective-permute-start.3
  228.5 7.9 collective-permute-start.4
  228.5 7.9 collective-permute-start.5
  236.4 7.9 collective-permute-start.6
  236.4 7.9 collective-permute-start.7
  244.3 7.8 collective-permute-start.8
  244.3 7.8 collective-permute-start.9
  252.1 8.4 collective-permute-start.10
  252.1 8.4 collective-permute-start.11
  260.5 8.1 collective-permute-start.12
  260.5 8.4 collective-permute-start.13
  268.6 8.5 collective-permute-start.14
  297.9 116.6 %all-gather.24.cloned.1.call-start = ((), (), s32[]{:S(2)}) async-start(), calls=%async_computation.18 | async-start | bytes 6684672 | tf_op jit(solution)/shard_map/all_gather | solution.py:277
  299.9 148.0 %all-gather.22.cloned.1.call-start = ((), (), s32[]{:S(2)}) async-start(), calls=%async_computation.17 | async-start | bytes 3145728 | tf_op jit(solution)/shard_map/all_gather | solution.py:107
  353.2 143.0 %all-gather.26.cloned.1.call-start = ((), (), s32[]{:S(2)}) async-start(), calls=%async_computation.19 | async-start | bytes 3342336 | tf_op jit(solution)/shard_map/all_gather | solution.py:278
  354.0 203.8 %reduce-scatter.14.cloned.1.call-start = ((), (), s32[]{:S(2)}) async-start(), calls=%async_computation.20 | async-start | bytes 6291456 | tf_op jit(solution)/shard_map/reduce_scatter | solution.py:111
  504.5 95.0 %all-gather.28.cloned.1.call-start = ((), (), s32[]{:S(2)}) async-start(), calls=%async_computation.21 | async-start | bytes 3145728 | tf_op jit(solution)/shard_map/all_gather | solution.py:107
  505.3 54.5 %copy-start.82 = (f32[2]{0:T(128)S(1)}, f32[2]{0:T(128)}, u32[]{:S(2)}) copy-start(f32[2]{0:T(128)} %copy-done.81) | copy-start | bytes 28
  505.4 54.5 %copy-start.83 = (f32[2]{0:T(128)S(1)}, f32[2]{0:T(128)}, u32[]{:S(2)}) copy-start(f32[2]{0:T(128)} %get-tuple-element.154) | copy-start | bytes 28
  566.3 111.8 %reduce-scatter.16.cloned.1.call-start = ((), (), s32[]{:S(2)}) async-start(), calls=%async_computation.22 | async-start | bytes 6291456 | tf_op jit(solution)/shard_map/reduce_scatter | solution.py:111
  623.6 94.8 %all-gather.30.cloned.1.call-start = ((), (), s32[]{:S(2)}) async-start(), calls=%async_computation.23 | async-start | bytes 3145728 | tf_op jit(solution)/shard_map/all_gather | solution.py:107
  685.1 81.6 %all-gather.32.cloned.1.call-start = ((), (), s32[]{:S(2)}) async-start(), calls=%async_computation.28 | async-start | bytes 3342336 | tf_op jit(solution)/shard_map/all_gather | solution.py:305
  685.7 36.3 %copy-start.37 = (f32[4,8,256]{2,1,0:T(8,128)S(1)}, f32[4,8,256]{2,1,0:T(8,128)}, u32[]{:S(2)}) copy-start(f32[4,8,256]{2,1,0:T(8,128)} %copy-done.36) | copy-start | bytes 98308
  685.7 141.9 %reduce-scatter.26.cloned.1.call-start = ((), (), s32[]{:S(2)}) async-start(), calls=%async_computation.29 | async-start | bytes 6291456 | tf_op jit(solution)/shard_map/reduce_scatter | solution.py:111
  741.0 25.7 %copy-start.31 = (bf16[4,256,1,512]{3,1,0,2:T(8,128)(2,1)S(1)}, bf16[4,256,1,512]{3,1,0,2:T(8,128)(2,1)}, u32[]{:S(2)}) copy-start(bf16[4,256,1,512]{3,1,0,2:T(8,128)(2,1)} %copy.165) | copy-start | bytes 3145732
  744.7 22.0 %copy-start.34 = (bf16[4,256,1,512]{3,1,0,2:T(8,128)(2,1)}, bf16[4,256,1,512]{3,1,0,2:T(8,128)(2,1)S(1)}, u32[]{:S(2)}) copy-start(bf16[4,256,1,512]{3,1,0,2:T(8,128)(2,1)S(1)} %copy.163) | copy-start | bytes 3145732
  774.3 142.3 %reduce-scatter.24.cloned.1.call-start = ((), (), s32[]{:S(2)}) async-start(), calls=%async_computation.27 | async-start | bytes 6684672 | tf_op jit(solution)/shard_map/reduce_scatter | solution.py:320
  783.3 5.5 copy-start.85
  783.3 198.3 %reduce-scatter.20.cloned.1.call-start = ((), (), s32[]{:S(2)}) async-start(), calls=%async_computation.25 | async-start | bytes 2228224 | tf_op jit(solution)/shard_map/reduce_scatter | solution.py:318
  788.7 330.5 %reduce-scatter.22.cloned.1.call-start = ((), (), s32[]{:S(2)}) async-start(), calls=%async_computation.26 | async-start | bytes 13369344 | tf_op jit(solution)/shard_map/reduce_scatter | solution.py:319
  801.4 406.2 %reduce-scatter.18.cloned.1.call-start = ((), (), s32[]{:S(2)}) async-start(), calls=%async_computation.24 | async-start | bytes 6684672 | tf_op jit(solution)/shard_map/reduce_scatter | solution.py:317
  810.3 17.3 %copy-start.6 = (f32[2,256,1024]{2,1,0:T(8,128)S(1)}, f32[2,256,1024]{2,1,0:T(8,128)}, u32[]{:S(2)}) copy-start(f32[2,256,1024]{2,1,0:T(8,128)} %copy-done.5) | copy-start | bytes 6291460
  810.3 17.3 %copy-start.63 = (f32[2,1,1024]{2,0,1:T(2,128)S(1)}, f32[2,1,1024]{2,0,1:T(2,128)}, u32[]{:S(2)}) copy-start(f32[2,1,1024]{2,0,1:T(2,128)} %copy-done.62) | copy-start | bytes 24580
  810.3 17.3 %copy-start.66 = (f32[2,256]{1,0:T(2,128)S(1)}, f32[2,256]{1,0:T(2,128)}, u32[]{:S(2)}) copy-start(f32[2,256]{1,0:T(2,128)} %copy-done.65) | copy-start | bytes 6148
  810.3 504.3 %reduce-scatter.30.cloned.1.call-start = ((), (), s32[]{:S(2)}) async-start(), calls=%async_computation.31 | async-start | bytes 3244032 | tf_op jit(solution)/shard_map/reduce_scatter | solution.py:333
  829.7 6.2 copy-start.53
  829.8 6.2 copy-start.57
  829.8 8.8 copy-start.78
  829.8 8.8 copy-start.70
  829.8 8.8 copy-start.76
  841.9 592.5 %reduce-scatter.28.cloned.1.call-start = ((), (), s32[]{:S(2)}) async-start(), calls=%async_computation.30 | async-start | bytes 6488064 | tf_op jit(solution)/shard_map/reduce_scatter | solution.py:332
  852.3 743.0 %reduce-scatter.32.cloned.1.call-start = ((), (), s32[]{:S(2)}) async-start(), calls=%async_computation.32 | async-start | bytes 12976128 | tf_op jit(solution)/shard_map/reduce_scatter | solution.py:334
  863.8 774.9 %copy-start.18 = (f32[64,2,1536]{2,1,0:T(2,128)S(1)}, f32[64,2,1536]{2,1,0:T(2,128)}, u32[]{:S(2)}) copy-start(f32[64,2,1536]{2,1,0:T(2,128)} %param.41) | copy-start | bytes 2359300
  863.8 774.9 %copy-start.40 = (f32[64,2,1536]{2,1,0:T(2,128)S(1)}, f32[64,2,1536]{2,1,0:T(2,128)}, u32[]{:S(2)}) copy-start(f32[64,2,1536]{2,1,0:T(2,128)} %param.43) | copy-start | bytes 2359300
  863.8 774.9 %copy-start.41 = (f32[64,2,1536]{2,1,0:T(2,128)S(1)}, f32[64,2,1536]{2,1,0:T(2,128)}, u32[]{:S(2)}) copy-start(f32[64,2,1536]{2,1,0:T(2,128)} %param.42) | copy-start | bytes 2359300
  1642.1 5.2 copy-start.25
  1642.1 5.2 copy-start.27
  (65 other events, 186.2 us)
Sparse Core Ops, SparseCore 0:
  11.5 61.7 all-gather.11
  76.8 68.2 all-gather.15
  148.6 53.5 all-gather.13
  211.6 31.9 all-gather.17
  246.2 40.3 all-gather.19
  298.0 51.3 reduce-scatter.11
  352.5 61.9 all-gather.23
  416.1 31.6 all-gather.21
  451.0 45.1 all-gather.25
  504.6 53.0 reduce-scatter.13
  566.4 33.1 all-gather.27
  623.7 54.2 reduce-scatter.15
  685.2 33.1 all-gather.29
  721.2 45.4 all-gather.31
  774.5 53.0 reduce-scatter.25
  831.4 85.2 reduce-scatter.23
  920.7 60.8 reduce-scatter.19
  985.5 133.6 reduce-scatter.21
  1123.2 84.3 reduce-scatter.17
  1213.7 100.8 reduce-scatter.29
  1321.2 113.1 reduce-scatter.27
  1440.4 154.9 reduce-scatter.31
